TPU v7x, 256 devices: a whole 4x4x8 slice. The times are simulated.
256 devices in a mesh: ri: 16 (over z, core), ao: 16 (over x, y).
Axes of the slice: x: 4, y: 4, z: 8, core: 2. Of those that a mesh axis runs over, the one named last changes fastest.
Arguments:
- three_center: bfloat16 [256, 2048, 2048], P('ri', 'ao'), as said below
- slab_tensor: bfloat16 [32, 2048, 2048], P('ri', 'ao'), as said below
- occ_green: bfloat16 [2048, 2048], P('ao'), as said below
- virt_green: bfloat16 [2048, 2048], P('ao'), as said below
- pattern: int32 [128, 128], replicated, may hold values from 0 to 1, as said below
- atom_sizes: int32 [128], replicated, may hold values from 6 to 16, as said below
Outputs:
- polar_slab: float32 [256, 32], P('ri')
Inputs may be any that keep to these rules, and one draw needn't show every extreme that they name: three_center is symmetric in its last two dimensions. slab_tensor is symmetric in its last two dimensions. `occ_green`: symmetric matrix. `virt_green`: symmetric matrix. `pattern`: symmetric 0/1 matrix with ones on the diagonal. `atom_sizes`: some atom block has all 16 functions live.
All inputs are finite; a program needn't handle non-finite values.
Results may differ from a plain program's by a relative error of at most 0.0041.
Values may be sent and summed in bfloat16 or wider, within the bound.
A program may use at most 128 MiB of HBM per device.

v0:
```python
import jax
import jax.numpy as jnp
from jax import lax
from jax.sharding import PartitionSpec as P

ATOM_BS = 16


def live_functions(atom_sizes):
    atom_count = atom_sizes.shape[0]
    per_slot = jnp.broadcast_to(atom_sizes[:, None], (atom_count, ATOM_BS)).reshape(-1)
    slot_ids = jnp.broadcast_to(
        jnp.arange(ATOM_BS, dtype=jnp.int32)[None, :], (atom_count, ATOM_BS)
    ).reshape(-1)
    return (slot_ids < per_slot).astype(jnp.float32)


def expand_pattern(pattern_rows):
    row_atoms = pattern_rows.shape[0]
    col_atoms = pattern_rows.shape[1]
    grown = jnp.broadcast_to(
        pattern_rows[:, None, :, None], (row_atoms, ATOM_BS, col_atoms, ATOM_BS)
    )
    return grown.reshape(row_atoms * ATOM_BS, col_atoms * ATOM_BS).astype(jnp.float32)


def shards(three_center, slab_tensor, occ_green, virt_green, pattern, atom_sizes):
    own_rows = occ_green.shape[0]
    ao_total = occ_green.shape[1]
    slab_rows = slab_tensor.shape[0]
    ri_rows = three_center.shape[0]
    ao_index = lax.axis_index("ao")
    live_mask = live_functions(atom_sizes)
    live_rows = lax.dynamic_slice_in_dim(live_mask, ao_index * own_rows, own_rows, 0)
    pattern_rows = lax.dynamic_slice_in_dim(
        pattern, ao_index * (own_rows // ATOM_BS), own_rows // ATOM_BS, 0
    )
    screen = (expand_pattern(pattern_rows) * live_rows[:, None] * live_mask[None, :]).astype(
        jnp.bfloat16
    )
    masked = three_center * screen[None]
    slab_masked = slab_tensor * screen[None]
    shard_piece = lax.all_gather(slab_masked, "ao", axis=1, tiled=True)
    left_product = jnp.einsum(
        "ml,qls->qms", occ_green, shard_piece, preferred_element_type=jnp.float32
    ).astype(jnp.bfloat16)
    left_flat = left_product.reshape(slab_rows * own_rows, ao_total)
    weighted = lax.dot_general(
        left_flat,
        lax.all_gather(virt_green, "ao", axis=0, tiled=True),
        (((1,), (1,)), ((), ())),
        preferred_element_type=jnp.float32,
    ).astype(jnp.bfloat16)
    weighted = weighted.reshape(slab_rows, own_rows, ao_total)
    flattened = masked.reshape(ri_rows, own_rows * ao_total)
    shard_piece = lax.all_gather(weighted, "ri", axis=0, tiled=True)
    piece_rows = shard_piece.shape[0]
    columns_part = lax.dot_general(
        flattened,
        shard_piece.reshape(piece_rows, own_rows * ao_total),
        (((1,), (1,)), ((), ())),
        preferred_element_type=jnp.float32,
    )
    return lax.psum(columns_part, "ao") / ao_total


def solution(mesh):
    placed = (P("ri", "ao", None), P("ri", "ao", None), P("ao", None), P("ao", None), P(), P())
    return jax.shard_map(
        shards, mesh=mesh, in_specs=placed, out_specs=P("ri", None), check_vma=False
    )
```

profile of v0, /device:TPU:1, one launch (start us, length us, event | category | flops | bytes accessed | tf_op | source)
XLA Modules:
  0.0 404.0 jit_solution(9870529525980081506)
XLA Ops:
  6.5 0.0 copy-start
  6.5 0.0 all-gather.4.cloned.1.call-start
  6.5 0.7 dynamic-slice_convert_fusion
  7.3 0.0 copy-start.3
  7.3 0.0 copy-start.2
  7.3 4.3 %broadcast_in_dim.6 = f32[8,16,128,16]{3,2,1,0:T(8,128)} broadcast(f32[8,128]{1,0:T(8,128)S(1)} %dynamic-slice_convert_fusion), dimensions={0,2} | broadcast | bytes 1052672 | tf_op jit(solution)/shard_map/broadcast_in_dim | solution.py:21
  11.6 7.9 %convert_element_type.38 = f32[128,2048]{1,0:T(8,128)S(1)} reshape(f32[8,16,128,16]{3,2,1,0:T(8,128)} %broadcast_in_dim.6) | data formatting | bytes 2097152 | tf_op jit(solution)/shard_map/convert_element_type | solution.py:24
  19.5 0.0 copy-done.3
  19.5 0.1 fusion.9
  19.6 0.1 reshape.62
  19.7 0.1 dynamic_slice.7
  19.7 0.2 multiply_convert_fusion
  19.9 0.0 copy-done.2
  19.9 1.2 broadcast_multiply_fusion.1
  21.1 0.0 all-gather.4.cloned.1.call-update
  21.1 0.0 all-gather.6.cloned.1.call-start
  21.2 0.7 all-gather.6.cloned.1.call-update
  21.9 0.0 all-gather.8.cloned.1.call-start
  21.9 119.5 %all-gather.4.cloned.1.call-done = bf16[2,2048,2048]{2,1,0:T(8,128)(2,1)} async-done(((bf16[2,128,2048]{2,1,0:T(8,128)(2,1)}), bf16[2,2048,2048]{2,1,0:T(8,128)(2,1)}) %all-gather.4.cloned.1.call-update) | async-done | bytes 16777232 | tf_op jit(solution)/shard_map/all_gather | solution.py:43
  141.4 0.0 copy-done
  141.4 8.1 %convolution_convert_fusion = bf16[2,2048,128]{1,2,0:T(8,128)(2,1)S(1)} fusion(bf16[2,2048,2048]{2,1,0:T(8,128)(2,1)} %all-gather.4.cloned.1.call-done, bf16[128,2048]{1,0:T(8,128)(2,1)S(1)} %copy-done), kind=kOutput, calls=%fused_computation.4 | convolution fusion | flops 2148007936 | bytes 18350080 | tf_op jit(solution)/shard_map/ml,qls->qms/dot_general | solution.py:44
  149.5 69.9 %all-gather.6.cloned.1.call-done = bf16[2048,2048]{1,0:T(8,128)(2,1)} async-done(((bf16[128,2048]{1,0:T(8,128)(2,1)}), bf16[2048,2048]{1,0:T(8,128)(2,1)}) %all-gather.6.cloned.1.call-update) | async-done | bytes 8388624 | tf_op jit(solution)/shard_map/all_gather | solution.py:50
  219.4 6.8 %convolution_convert_fusion.1 = bf16[256,2048]{1,0:T(8,128)(2,1)} fusion(bf16[256,2048]{1,0:T(8,128)(2,1)S(1)} %bitcast.14, bf16[2048,2048]{1,0:T(8,128)(2,1)} %all-gather.6.cloned.1.call-done), kind=kOutput, calls=%fused_computation.5 | convolution fusion | flops 2148007936 | bytes 10485760 | tf_op jit(solution)/shard_map/dot_general | solution.py:48
  226.2 0.0 all-gather.8.cloned.1.call-update
  226.2 7.4 %broadcast_multiply_fusion = bf16[16,128,2048]{2,1,0:T(8,128)(2,1)} fusion(bf16[16,128,2048]{2,1,0:T(8,128)(2,1)} %param.6, bf16[128,2048]{1,0:T(8,128)(2,1)S(1)} %multiply_convert_fusion), kind=kLoop, calls=%fused_computation.3 | loop fusion | flops 4194304 | bytes 17301504 | tf_op jit(solution)/shard_map/mul | solution.py:41
  233.7 88.3 %all-gather.8.cloned.1.call-done = bf16[32,128,2048]{2,1,0:T(8,128)(2,1)} async-done(((bf16[2,128,2048]{2,1,0:T(8,128)(2,1)}), bf16[32,128,2048]{2,1,0:T(8,128)(2,1)}) %all-gather.8.cloned.1.call-update) | async-done | bytes 16777232 | tf_op jit(solution)/shard_map/all_gather | solution.py:56
  321.9 0.0 copy-start.1
  321.9 41.2 %fusion.3 = f32[16,32]{1,0:T(8,128)S(1)} fusion(bf16[32,128,2048]{2,1,0:T(8,128)(2,1)} %all-gather.8.cloned.1.call-done, bf16[16,128,2048]{2,1,0:T(8,128)(2,1)} %broadcast_multiply_fusion), kind=kOutput, calls=%fused_computation.6 | convolution fusion | flops 268435456 | bytes 25167872 | tf_op jit(solution)/shard_map/dot_general | solution.py:58
  363.1 33.7 %psum.7 = f32[16,32]{1,0:T(8,128)S(1)} all-reduce(f32[16,32]{1,0:T(8,128)S(1)} %fusion.3), channel_id=1, replica_groups=mesh['ri'=16,'ao'=16] {'ao'}, use_global_device_ids=true, to_apply=%region_0.0 | all-reduce | flops 512 | bytes 4096 | tf_op jit(solution)/shard_map/psum | solution.py:64
  396.8 0.6 broadcast_multiply_fusion.2
  397.4 0.0 copy-done.1
Async XLA Ops:
  6.5 134.8 %copy-start = (bf16[128,2048]{1,0:T(8,128)(2,1)S(1)}, bf16[128,2048]{1,0:T(8,128)(2,1)}, u32[]{:S(2)}) copy-start(bf16[128,2048]{1,0:T(8,128)(2,1)} %param.8) | copy-start | bytes 1572868
  6.5 134.8 %all-gather.4.cloned.1.call-start = ((), (), s32[]{:S(2)}) async-start(), calls=%async_computation | async-start | bytes 17825792 | tf_op jit(solution)/shard_map/all_gather | solution.py:43
  7.3 12.2 %copy-start.3 = (s32[128]{0:T(128)S(1)}, s32[128]{0:T(128)}, u32[]{:S(2)}) copy-start(s32[128]{0:T(128)} %param.11) | copy-start | bytes 1540
  7.3 12.6 %copy-start.2 = (bf16[2,128,2048]{2,1,0:T(8,128)(2,1)S(1)}, bf16[2,128,2048]{2,1,0:T(8,128)(2,1)}, u32[]{:S(2)}) copy-start(bf16[2,128,2048]{2,1,0:T(8,128)(2,1)} %param.7) | copy-start | bytes 3145732
  21.1 198.3 %all-gather.6.cloned.1.call-start = ((), (), s32[]{:S(2)}) async-start(), calls=%async_computation.1 | async-start | bytes 8912896 | tf_op jit(solution)/shard_map/all_gather | solution.py:50
  21.9 300.1 %all-gather.8.cloned.1.call-start = ((), (), s32[]{:S(2)}) async-start(), calls=%async_computation.2 | async-start | bytes 17825792 | tf_op jit(solution)/shard_map/all_gather | solution.py:56
  321.9 75.5 %copy-start.1 = (bf16[128,2048]{1,0:T(8,128)(2,1)S(1)}, bf16[128,2048]{1,0:T(8,128)(2,1)}, u32[]{:S(2)}) copy-start(bf16[128,2048]{1,0:T(8,128)(2,1)} %param.8) | copy-start | bytes 1572868
Sparse Core Ops, SparseCore 0:
  21.2 120.0 all-gather.3
  143.8 75.5 all-gather.5
  226.3 95.5 all-gather.7
where the time goes:
time: 408 us; the launch traced here: 404 us
  waiting for transfers between devices  278 us (68%)
  matrix products  56.1 us (14%)
  blocking collectives  33.7 us (8%)
  between operations  13.2 us (3%)
  local copies, waits for them, and re-layouts  12.4 us (3%)
  other arithmetic  10.2 us (2%)
    all_gather x1, waiting for transfers between devices, shards(): shard_piece = lax.all_gather(slab_masked, 'ao', axis=1, tiled=True)  119 us
    all_gather x1, waiting for transfers between devices, shards(): shard_piece = lax.all_gather(weighted, 'ri', axis=0, tiled=True)  88.3 us
    all_gather x1, waiting for transfers between devices, shards(): lax.all_gather(virt_green, 'ao', axis=0, tiled=True)  69.9 us
    dot_general x1, matrix products, shards(): lax.dot_general(flattened, shard_piece.reshape(piece_rows, own_rows * ao_...  41.2 us
    psum x1, blocking collectives, shards(): return lax.psum(columns_part, 'ao') / ao_total  33.7 us
  transfers between devices with their start and end apart: 3, of which 3 were waited for; matrix products, arithmetic and copies ran while one was open for 4% of the time, Pallas kernels for 0%

commit v1 on v0

v1 whole, which is shorter than its diff:
```python
import functools

import jax
import jax.numpy as jnp
from jax import lax
from jax.experimental import pallas as pl
from jax.experimental.pallas import tpu as pltpu
from jax.sharding import PartitionSpec as P

MESH = pl.DeviceIdType.MESH
ATOM_BS = 16
NX, NY, NZ = 4, 4, 8
ROWS = 16

MIRRORED = ((1, 0), (1, 1), (1, 2), (1, 3), (0, 1), (2, 1))
PLAIN = ((0, 0), (0, 2), (2, 0), (2, 2))
OWNED = MIRRORED + PLAIN
NT = (((1,), (1,)), ((), ()))


def kernel(
    m_ref, s_ref, o_ref, v_ref, pat_ref, size_ref, out_ref,
    oh, vn, sg, lb, wb, fx1, fx2, tb, wz, mb, scr, part, red_s, red_x, red_y,
    ssem, rsem, lsem,
):
    blk, ao_total = o_ref.shape
    ri_rows = m_ref.shape[0]
    ri, ao = lax.axis_index("ri"), lax.axis_index("ao")
    z, core = ri // 2, ri % 2
    x, y = ao // NY, ao % NY

    def at_x(d):
        return (x + d) % NX

    def at_y(d):
        return (y + d) % NY

    def at_z(d):
        return (z + d) % NZ

    def dev(dx=0, dy=0, dz=0):
        return (at_z(dz) * 2 + core, at_x(dx) * NY + at_y(dy))

    sibling = (z * 2 + 1 - core, ao)
    half = blk // 2
    mine = pl.ds(pl.multiple_of(core * half, half), half)

    sent = []

    def send(src, dst, device):
        slot = len(sent)
        copy = pltpu.make_async_remote_copy(
            src_ref=src, dst_ref=dst, send_sem=ssem.at[slot], recv_sem=rsem.at[slot],
            device_id=device, device_id_type=MESH,
        )
        copy.start()
        sent.append(copy)
        return slot

    def arrived(ref, slot):
        pltpu.make_async_remote_copy(
            src_ref=ref, dst_ref=ref, send_sem=ssem.at[slot], recv_sem=rsem.at[slot],
            device_id=sibling, device_id_type=MESH,
        ).wait_recv()

    barrier = pltpu.get_barrier_semaphore()
    partners = [dev(dx=1), dev(dx=2), dev(dx=3), dev(dy=1), dev(dy=2), dev(dy=3), dev(dz=1), dev(dz=7), sibling]
    for partner in partners:
        pl.semaphore_signal(barrier, inc=1, device_id=partner, device_id_type=MESH)
    pl.semaphore_wait(barrier, len(partners))

    class Ring:
        def __init__(self, view, at, device, rows, start=0):
            self.view, self.at, self.device = view, at, device
            self.low = pl.ds(start, rows // 2)
            self.high = pl.ds(start + rows // 2, rows // 2)
            self.all = pl.ds(start, rows)

        def start(self, src=None):
            block = self.view(self.at(0), self.all)
            src = block if src is None else src
            self.a = send(src, block, self.device(1))
            self.b = send(src, block, self.device(3))

        def forward(self):
            arrived(self.view(self.at(3), self.all), self.a)
            piece = self.view(self.at(3), self.low)
            self.c = send(piece, piece, self.device(1))
            arrived(self.view(self.at(1), self.all), self.b)
            piece = self.view(self.at(1), self.high)
            self.d = send(piece, piece, self.device(3))

        def finish(self):
            arrived(self.view(self.at(2), self.low), self.c)
            arrived(self.view(self.at(2), self.high), self.d)

    def along_x(d):
        return dev(dx=d)

    def along_y(d):
        return dev(dy=d)

    class Shared(Ring):
        def share(self, d):
            piece = self.view(self.at(d), self.all)
            return send(piece, piece, sibling)

        def forward(self):
            super().forward()
            self.shared = [self.share(3), self.share(1)]

        def finish(self):
            super().finish()
            self.shared.append(self.share(2))

        def join(self):
            other = pl.ds(pl.multiple_of((1 - core) * half, half), half)
            for d, slot in zip((3, 1, 2), self.shared):
                arrived(self.view(self.at(d), other), slot)

    base = pl.multiple_of(core * half, half)
    o_ring = Shared(lambda i, r: oh.at[i, r], at_x, along_x, half, base)
    v_ring = Shared(lambda i, r: vn.at[i, r], at_y, along_y, half, base)
    s_rings = [Ring(lambda i, r, q=q: sg.at[q, i, r], at_y, along_y, blk) for q in range(2)]
    l_rings = [Ring(lambda i, r, q=q: lb.at[q, i, r], at_x, along_x, NX * blk) for q in range(2)]

    o_ring.start(o_ref.at[mine])

    atoms = pat_ref.shape[0]
    sizes = size_ref[...]
    row = lax.broadcasted_iota(jnp.int32, (blk, atoms), 0) + ao * blk
    row = row - lax.broadcasted_iota(jnp.int32, (blk, atoms), 1) * ATOM_BS
    grow_rows = jnp.where((row >= 0) & (row < sizes), 1.0, 0.0).astype(jnp.bfloat16)
    col = lax.broadcasted_iota(jnp.int32, (ao_total, atoms), 0)
    col = col - lax.broadcasted_iota(jnp.int32, (ao_total, atoms), 1) * ATOM_BS
    grow_cols = jnp.where((col >= 0) & (col < sizes), 1.0, 0.0).astype(jnp.bfloat16)
    pat = pat_ref[...].astype(jnp.float32).astype(jnp.bfloat16)
    pat_rows = jnp.dot(grow_rows, pat, preferred_element_type=jnp.float32).astype(jnp.bfloat16)
    screen = lax.dot_general(pat_rows, grow_cols, NT, preferred_element_type=jnp.float32)
    for b in range(NX * NY):
        scr[b] = screen[:, b * blk:(b + 1) * blk]
    for q in range(2):
        for b in range(NX * NY):
            cols = slice(b * blk, (b + 1) * blk)
            sg[q, y, :, cols] = (s_ref[q, :, cols].astype(jnp.float32) * scr[b]).astype(jnp.bfloat16)
        if q == 0:
            s_rings[0].start()

    locals_, m_slots = [], []
    for k, (dx, dy) in enumerate(OWNED):
        b = at_x(dx) * NY + at_y(dy)
        src = m_ref.at[:, :, pl.ds(pl.multiple_of(b * blk, blk), blk)]
        copy = pltpu.make_async_copy(src, mb.at[pl.ds(0, ri_rows), :, pl.ds(k * blk, blk)], lsem.at[k])
        copy.start()
        locals_.append(copy)
        m_slots.append(send(src, mb.at[pl.ds(ri_rows, ri_rows), :, pl.ds(k * blk, blk)], sibling))

    oh[x] = o_ref[...]
    vn[y] = v_ref[...]

    def left(q):
        product = lax.dot_general(
            oh[...].reshape(NX * blk, ao_total), sg[q].reshape(NY * blk, ao_total), NT,
            preferred_element_type=jnp.float32,
        )
        lb[q, x] = product.astype(jnp.bfloat16)

    def weighted(q):
        rows = jnp.concatenate([lb[q, i] for i in range(NX)], axis=1)
        product = lax.dot_general(
            rows, vn[...].reshape(NY * blk, ao_total), NT, preferred_element_type=jnp.float32
        ).astype(jnp.bfloat16)
        for i in range(NX):
            for j in range(NY):
                wb[q, i, j] = product[i * blk:(i + 1) * blk, j * blk:(j + 1) * blk]

    a_slots = {}

    def exchange(q):
        slots = {"x1": send(wb.at[q, at_x(3)], fx1.at[q], dev(dx=3))}
        for k, dy in enumerate((0, 1, 2)):
            slots["x2", k] = send(wb.at[q, at_x(2), at_y(dy)], fx2.at[q, k], dev(dx=2))
        for k, (dx, dy) in enumerate(MIRRORED):
            if dy:
                slots["t", k] = send(wb.at[q, at_x(dx), at_y(-dy % NY)], tb.at[q, k], dev(dy=-dy % NY))
        a_slots[q] = slots

    def assemble(q):
        slots = a_slots[q]
        arrived(fx1.at[q], slots["x1"])
        for k in range(3):
            arrived(fx2.at[q, k], slots["x2", k])
        for k, (dx, dy) in enumerate(MIRRORED):
            if dy:
                arrived(tb.at[q, k], slots["t", k])
        for k, (dx, dy) in enumerate(OWNED):
            if dx == 0:
                block = wb[q, x, at_y(dy)]
            elif dx == 1:
                block = fx1[q, at_y(dy)]
            else:
                block = fx2[q, dy]
            block = block.astype(jnp.float32)
            if k < len(MIRRORED):
                mirror = tb[q, k] if dy else wb[q, at_x(dx), y]
                block = block + mirror.astype(jnp.float32).T
            block = block * scr[at_x(dx) * NY + at_y(dy)]
            wz[z, q, :, k * blk:(k + 1) * blk] = block.astype(jnp.bfloat16)

    calls = []

    def contract(q, offsets):
        number = len(calls)
        width = ROWS * len(offsets)

        def step(i, total):
            rows = pl.ds(pl.multiple_of(i * ROWS, ROWS), ROWS)
            a = mb[:, rows, :].reshape(2 * ri_rows * ROWS, mb.shape[2])
            b = jnp.concatenate([wz[at_z(d), q, rows, :] for d in offsets], axis=0)
            return total + lax.dot_general(a, b, NT, preferred_element_type=jnp.float32)

        total = lax.fori_loop(0, blk // ROWS, step, jnp.zeros((2 * ri_rows * ROWS, width), jnp.float32))
        i = lax.broadcasted_iota(jnp.int32, total.shape, 0) % ROWS
        j = lax.broadcasted_iota(jnp.int32, total.shape, 1)
        total = jnp.where(i == j % ROWS, total, 0.0)
        total = jnp.sum(total.reshape(2 * ri_rows, ROWS, width), axis=1)
        unit = lax.broadcasted_iota(jnp.int32, (width, 128), 0) // ROWS
        column = lax.broadcasted_iota(jnp.int32, (width, 128), 1)
        place = jnp.zeros((width, 128), jnp.float32)
        for u, d in enumerate(offsets):
            place = jnp.where((unit == u) & (column == 4 * at_z(d) + 2 * core + q), 1.0, place)
        term = jnp.dot(total, place, precision=lax.Precision.HIGHEST, preferred_element_type=jnp.float32)
        part[...] = term if number == 0 else part[...] + term
        calls.append(number)

    z_slots = [{}, {}]

    def z_send(q, k):
        up, down = wz.at[at_z(1 - k), q], wz.at[at_z(k - 1), q]
        if k == NZ // 2:
            up = wz.at[at_z(1 - k), q, pl.ds(0, half)]
            down = wz.at[at_z(k - 1), q, pl.ds(half, half)]
        z_slots[q][k] = send(up, up, dev(dz=1)), send(down, down, dev(dz=7))

    def z_arrived(q, k):
        low, high = z_slots[q][k]
        if k == NZ // 2:
            arrived(wz.at[at_z(k), q, pl.ds(0, half)], low)
            arrived(wz.at[at_z(k), q, pl.ds(half, half)], high)
        else:
            arrived(wz.at[at_z(-k), q], low)
            arrived(wz.at[at_z(k), q], high)

    o_ring.forward()
    s_rings[0].forward()
    v_ring.start(v_ref.at[mine])
    s_rings[1].start()
    o_ring.finish()
    s_rings[0].finish()
    o_ring.join()
    left(0)
    l_rings[0].start()
    v_ring.forward()
    s_rings[1].forward()
    l_rings[0].forward()
    v_ring.finish()
    s_rings[1].finish()
    left(1)
    l_rings[1].start()
    v_ring.join()
    l_rings[0].finish()
    weighted(0)
    exchange(0)
    l_rings[1].forward()
    assemble(0)
    z_send(0, 1)
    for copy in locals_:
        copy.wait()
    for k, slot in enumerate(m_slots):
        arrived(mb.at[pl.ds(ri_rows, ri_rows), :, pl.ds(k * blk, blk)], slot)
    contract(0, (0,))
    l_rings[1].finish()
    weighted(1)
    exchange(1)
    z_arrived(0, 1)
    z_send(0, 2)
    assemble(1)
    z_send(1, 1)
    contract(1, (0,))
    contract(0, (7, 1))
    for k in range(2, NZ // 2 + 1):
        z_arrived(0, k)
        if k < NZ // 2:
            z_send(0, k + 1)
        z_arrived(1, k - 1)
        z_send(1, k)
        contract(0, (NZ - k, k) if k < NZ // 2 else (k,))
        contract(1, (NZ - k + 1, k - 1))
    z_arrived(1, NZ // 2)
    contract(1, (NZ // 2,))

    slot = send(part.at[pl.ds(ri_rows, ri_rows)], red_s, sibling)
    arrived(red_s, slot)
    red_x[x] = part[:ri_rows] + red_s[...]
    slots = [send(red_x.at[x], red_x.at[x], dev(dx=d)) for d in (1, 2, 3)]
    for d, slot in zip((1, 2, 3), slots):
        arrived(red_x.at[at_x(-d % NX)], slot)
    red_y[y] = red_x[0] + red_x[1] + red_x[2] + red_x[3]
    slots = [send(red_y.at[y], red_y.at[y], dev(dy=d)) for d in (1, 2, 3)]
    for d, slot in zip((1, 2, 3), slots):
        arrived(red_y.at[at_y(-d % NY)], slot)
    total = red_y[0] + red_y[1] + red_y[2] + red_y[3]
    out_ref[...] = total[:, :out_ref.shape[1]] / ao_total
    for copy in sent:
        copy.wait_send()


def shards(three_center, slab_tensor, occ_green, virt_green, pattern, atom_sizes):
    ri_rows, blk, ao_total = three_center.shape
    n_owned, n_mirrored = len(OWNED), len(MIRRORED)
    bf16, f32 = jnp.bfloat16, jnp.float32
    vmem = pl.BlockSpec(memory_space=pltpu.VMEM)
    columns = 4 * NZ
    return pl.pallas_call(
        kernel,
        out_shape=jax.ShapeDtypeStruct((ri_rows, columns), f32),
        in_specs=[pl.BlockSpec(memory_space=pl.ANY)] + [vmem] * 5,
        out_specs=vmem,
        scratch_shapes=[
            pltpu.VMEM((NX, blk, ao_total), bf16),
            pltpu.VMEM((NY, blk, ao_total), bf16),
            pltpu.VMEM((2, NY, blk, ao_total), bf16),
            pltpu.VMEM((2, NX, NX * blk, NY * blk), bf16),
            pltpu.VMEM((2, NX, NY, blk, blk), bf16),
            pltpu.VMEM((2, NY, blk, blk), bf16),
            pltpu.VMEM((2, 3, blk, blk), bf16),
            pltpu.VMEM((2, n_mirrored, blk, blk), bf16),
            pltpu.VMEM((NZ, 2, blk, n_owned * blk), bf16),
            pltpu.VMEM((2 * ri_rows, blk, n_owned * blk), bf16),
            pltpu.VMEM((NX * NY, blk, blk), f32),
            pltpu.VMEM((2 * ri_rows, 128), f32),
            pltpu.VMEM((ri_rows, 128), f32),
            pltpu.VMEM((NX, ri_rows, 128), f32),
            pltpu.VMEM((NY, ri_rows, 128), f32),
            pltpu.SemaphoreType.DMA((96,)),
            pltpu.SemaphoreType.DMA((96,)),
            pltpu.SemaphoreType.DMA((n_owned,)),
        ],
        compiler_params=pltpu.CompilerParams(
            collective_id=0, has_side_effects=True, vmem_limit_bytes=60 * 1024 * 1024
        ),
        name="polar_slab",
    )(three_center, slab_tensor, occ_green, virt_green, pattern, atom_sizes.reshape(1, -1))


def solution(mesh):
    placed = (P("ri", "ao", None), P("ri", "ao", None), P("ao", None), P("ao", None), P(), P())
    return jax.shard_map(
        shards, mesh=mesh, in_specs=placed, out_specs=P("ri", None), check_vma=False
    )
```

time: 408 us -> 147 us (0.36); the launches traced: 404 us -> 147 us
  waiting for transfers between devices: 278 us -> 0 us
  Pallas kernels: 0 us -> 146 us
  matrix products: 56.1 us -> 0 us
  blocking collectives: 33.7 us -> 0 us
  between operations: 13.2 us -> 0.01 us
  local copies, waits for them, and re-layouts: 12.4 us -> 1.3 us
  other arithmetic: 10.2 us -> 0 us
    all_gather x3 -> x0, waiting for transfers between devices: 278 us -> none  [the longest x1 119 us: shards(): shard_piece = lax.all_gather(slab_masked, 'ao', axis=1, tiled=True)]
    pallas_call x0 -> x1, Pallas kernels: none -> 146 us  [shards(): pl.pallas_call(kernel, out_shape=jax.ShapeDtypeStruct((ri_rows, columns),...]
    dot_general x3 -> x0, matrix products: 56.1 us -> none  [the longest x1 41.2 us: shards(): lax.dot_general(flattened, shard_piece.reshape(piece_rows, own_rows * ao_...]
    psum x1 -> x0, blocking collectives: 33.7 us -> none  [shards(): return lax.psum(columns_part, 'ao') / ao_total]
    mul x2 -> x0, other arithmetic: 8.62 us -> none  [the longest x1 7.44 us: shards(): masked = three_center * screen[None]]
    convert_element_type x2 -> x0, local copies, waits for them, and re-layouts: 7.95 us -> none  [the longest x1 7.87 us: expand_pattern(): grown.reshape(row_atoms * ATOM_BS, col_atoms * ATOM_BS).astype(jnp.float32)]
    broadcast_in_dim x1 -> x0, local copies, waits for them, and re-layouts: 4.33 us -> none  [expand_pattern(): jnp.broadcast_to(pattern_rows[:, None, :, None], (row_atoms, ATOM_BS, col...]
  transfers between devices with their start and end apart: 3 -> 0, of which waited for: 3 -> 0; matrix products, arithmetic and copies ran while one was open for 4% -> 0% of each run, Pallas kernels for 0% -> 0%
where the time goes in v1:
time: 147 us
  Pallas kernels  146 us (99%)
    pallas_call x1, Pallas kernels, shards(): pl.pallas_call(kernel, out_shape=jax.ShapeDtypeStruct((ri_rows, columns),...  146 us

profile of v1, /device:TPU:1, one launch (start us, length us, event | category | flops | bytes accessed | tf_op | source)
XLA Modules:
  0.0 147.3 jit_solution(7762104190656235607)
XLA Ops:
  0.0 146.0 %polar_slab.1 = f32[16,32]{1,0:T(8,128)} custom-call(bf16[16,128,2048]{2,1,0:T(8,128)(2,1)} %m_ref.1, bf16[2,128,2048]{2,1,0:T(8,128)(2,1)} %s_ref.1, bf16[128,2048]{1,0:T(8,128)(2,1)} %o_ref.1, bf16[128,2048]{1,0:T(8,128)(2,1)} %v_ref.1, s32[128,128]{1,0:T(8,128)} %pat_ref.1, s32[1,128]{1,0:T(1,128)} %bitcast.1), custom_call_target="tpu_custom_call" | custom-call | tf_op jit(solution)/shard_map/polar_slab/pallas_call | solution.py:324
  146.0 1.3 copy.8

commit v2 on v0

v2 whole, which is shorter than its diff:
```python
import functools

import jax
import jax.numpy as jnp
from jax import lax
from jax.experimental import pallas as pl
from jax.experimental.pallas import tpu as pltpu
from jax.sharding import PartitionSpec as P

MESH = pl.DeviceIdType.MESH
ATOM_BS = 16
NX, NY, NZ = 4, 4, 8
ROWS = 16
CHUNKS = 4
SEMS = 96
V_PARTS = 4

MIRRORED = ((1, 0), (3, 3), (1, 3), (3, 2), (0, 1), (2, 1))
N_MAIN = len(MIRRORED) + 2
N_OWNED = N_MAIN + 1
TRAVEL = 6
NT = (((1,), (1,)), ((), ()))


def kernel(
    m_ref, s_ref, o_ref, v_ref, pat_ref, size_ref, out_ref,
    oh, vn, sg, lb, wb, ab0, ab1, wz0, wz1, mb, scr, gram, part, red_x, red_y,
    ssem, rsem, lsem,
):
    blk, ao_total = o_ref.shape
    ri_rows = m_ref.shape[0]
    ri, ao = lax.axis_index("ri"), lax.axis_index("ao")
    z, core = ri // 2, ri % 2
    x, y = ao // NY, ao % NY

    def at_x(d):
        return (x + d) % NX

    def at_y(d):
        return (y + d) % NY

    def at_z(d):
        return (z + d) % NZ

    def dev(dx=0, dy=0, dz=0):
        return (at_z(dz) * 2 + core, at_x(dx) * NY + at_y(dy))

    def other_core(dx):
        return (z * 2 + 1 - core, at_x(dx) * NY + y)

    sibling = (z * 2 + 1 - core, ao)
    half = blk // 2
    mine = pl.ds(pl.multiple_of(core * half, half), half)

    sent = []

    def remote(src, dst, device, slot):
        return pltpu.make_async_remote_copy(
            src_ref=src, dst_ref=dst, send_sem=ssem.at[slot], recv_sem=rsem.at[slot],
            device_id=device, device_id_type=MESH,
        )

    def group(whole):
        sent.append(remote(whole, whole, sibling, len(sent)))
        return len(sent) - 1

    def send(src, dst, device, slot=None):
        if slot is None:
            slot = len(sent)
            sent.append(remote(src, dst, device, slot))
        remote(src, dst, device, slot).start()
        return slot

    flushed = [0]

    def flush(keep=0):
        for copy in sent[flushed[0]:len(sent) - keep]:
            copy.wait_send()
        flushed[0] = len(sent) - keep

    def arrived(ref, slot):
        remote(ref, ref, sibling, slot).wait_recv()

    barrier = pltpu.get_barrier_semaphore()
    partners = [dev(dx=1), dev(dx=2), dev(dx=3), dev(dy=1), dev(dy=2), dev(dy=3), sibling]
    partners += [dev(dz=1), dev(dz=7)]
    partners += [other_core(1), other_core(2), other_core(3)]
    for partner in partners:
        pl.semaphore_signal(barrier, inc=1, device_id=partner, device_id_type=MESH)

    class Ring:
        def __init__(self, view, at, device, rows, start=0):
            self.view, self.at, self.device = view, at, device
            self.low = pl.ds(start, rows // 2)
            self.high = pl.ds(start + rows // 2, rows // 2)
            self.all = pl.ds(start, rows)

        def start(self, src=None):
            block = self.view(self.at(0), self.all)
            src = block if src is None else src
            self.a = send(src, block, self.device(1))
            self.b = send(src, block, self.device(3))

        def forward(self):
            arrived(self.view(self.at(3), self.all), self.a)
            piece = self.view(self.at(3), self.low)
            self.c = group(self.view(self.at(2), self.all))
            send(piece, piece, self.device(1), self.c)
            arrived(self.view(self.at(1), self.all), self.b)
            piece = self.view(self.at(1), self.high)
            send(piece, piece, self.device(3), self.c)

        def finish(self):
            arrived(self.view(self.at(2), self.all), self.c)

    def along_x(d):
        return dev(dx=d)

    def along_y(d):
        return dev(dy=d)

    base = pl.multiple_of(core * half, half)
    other = pl.ds(pl.multiple_of((1 - core) * half, half), half)
    v_width = ao_total // V_PARTS

    def v_part(i):
        return pl.ds(pl.multiple_of(i * v_width, v_width), v_width)

    v_cols = v_part(z % V_PARTS)
    c_rows = blk // CHUNKS
    n_chunks = 2 * CHUNKS

    o_ring = Ring(lambda i, r: oh.at[i, r], at_x, along_x, half, base)
    v_ring = Ring(lambda i, r: vn.at[i, r, v_cols], at_y, along_y, half, base)
    vz_ring = Ring(
        lambda i, r: vn.at[:, r, v_part(i)], lambda d: (z + d) % V_PARTS,
        lambda d: dev(dz=1 if d == 1 else NZ - 1), half, base,
    )
    s_rings, l_rings = [], []
    for t in range(n_chunks):
        q, start = t // CHUNKS, t % CHUNKS * c_rows
        s_rings.append(Ring(lambda i, r, q=q: sg.at[q, i, r], at_y, along_y, c_rows, start))
        l_rings.append(
            Ring(lambda i, r, q=q, start=start: lb.at[q, i, r, pl.ds(start, c_rows)], at_x, along_x, NY)
        )

    atoms = pat_ref.shape[0]
    sizes = size_ref[...]
    row = lax.broadcasted_iota(jnp.int32, (blk, atoms), 0) + ao * blk
    row = row - lax.broadcasted_iota(jnp.int32, (blk, atoms), 1) * ATOM_BS
    grow_rows = jnp.where((row >= 0) & (row < sizes), 1.0, 0.0).astype(jnp.bfloat16)
    col = lax.broadcasted_iota(jnp.int32, (ao_total, atoms), 0)
    col = col - lax.broadcasted_iota(jnp.int32, (ao_total, atoms), 1) * ATOM_BS
    grow_cols = jnp.where((col >= 0) & (col < sizes), 1.0, 0.0).astype(jnp.bfloat16)
    pat = pat_ref[...].astype(jnp.float32).astype(jnp.bfloat16)
    pat_rows = jnp.dot(grow_rows, pat, preferred_element_type=jnp.float32).astype(jnp.bfloat16)
    screen = lax.dot_general(pat_rows, grow_cols, NT, preferred_element_type=jnp.float32)
    for b in range(NX * NY):
        scr[b] = screen[:, b * blk:(b + 1) * blk]

    def mask(q):
        for b in range(NX * NY):
            cols = slice(b * blk, (b + 1) * blk)
            sg[q, y, :, cols] = (s_ref[q, :, cols].astype(jnp.float32) * scr[b]).astype(jnp.bfloat16)

    mask(0)
    oh[x] = o_ref[...]
    v_own = pltpu.make_async_copy(v_ref.at[mine, v_cols], vn.at[y, mine, v_cols], lsem.at[1])
    v_own.start()

    o_slots, v_slots, m_slots = [], [], []

    def o_share(d):
        piece = oh.at[at_x(d), mine]
        o_slots.append(send(piece, piece, sibling))

    def o_join():
        for d, slot in zip((3, 1, 2), o_slots):
            arrived(oh.at[at_x(d), other], slot)

    def v_share():
        piece = vn.at[:, mine]
        v_slots.append(send(piece, piece, sibling))

    def v_join():
        arrived(vn.at[:, other], v_slots[-1])

    far_x = at_x(2 * (y // 2))
    far_q = x // 2
    blocks = [at_x(dx) * NY + at_y(dy) for dx, dy in MIRRORED + ((0, 0),)]
    blocks += [far_x * NY + at_y(2), at_x(2) * NY + y]
    m_own, m_other = mb.at[pl.ds(0, ri_rows)], mb.at[pl.ds(ri_rows, ri_rows)]

    def m_start():
        m_slots.append(group(m_other))
        for k, b in enumerate(blocks):
            src = m_ref.at[:, :, pl.ds(pl.multiple_of(b * blk, blk), blk)]
            cols = pl.ds(k * blk, blk)
            pltpu.make_async_copy(src, mb.at[pl.ds(0, ri_rows), :, cols], lsem.at[0]).start()
            send(src, mb.at[pl.ds(ri_rows, ri_rows), :, cols], sibling, m_slots[0])

    def m_join():
        pltpu.make_async_copy(m_own, m_own, lsem.at[0]).wait()
        arrived(m_other, m_slots[0])

    def left(t):
        q, rows = t // CHUNKS, pl.ds(t % CHUNKS * c_rows, c_rows)
        product = lax.dot_general(
            sg[q, :, rows, :].reshape(NY * c_rows, ao_total), oh[...].reshape(NX * blk, ao_total), NT,
            preferred_element_type=jnp.float32,
        )
        lb[q, x, :, rows, :] = product.astype(jnp.bfloat16).reshape(NY, c_rows, NX * blk)

    def weighted(q):
        product = jnp.dot(
            vn[...].reshape(NY * blk, ao_total), lb[q].reshape(ao_total, NX * blk),
            preferred_element_type=jnp.float32,
        ).astype(jnp.bfloat16)
        for i in range(NX):
            for j in range(NY):
                wb[q, i, j] = product[j * blk:(j + 1) * blk, i * blk:(i + 1) * blk]

    a_slots = {}
    travel = (ab0, ab1)
    wz = (wz0, wz1)

    def exchange(q):
        slot = a_slots[q] = group(travel[q])
        along_x_, along_y_ = 0, TRAVEL
        for dx, dy in MIRRORED:
            if dx:
                send(wb.at[q, at_x(NX - dx), at_y(dy)], travel[q].at[along_x_], dev(dx=NX - dx), slot)
                along_x_ += 1
            if dy:
                send(wb.at[q, at_x(dx), at_y(NY - dy)], travel[q].at[along_y_], dev(dy=NY - dy), slot)
                along_y_ += 1
        send(wb.at[q, at_x(2), at_y(2)], travel[q].at[along_x_], dev(dx=2), slot)
        send(wb.at[q, at_x(2 - 2 * (y // 2)), at_y(2)], travel[q].at[along_y_], dev(dy=2), slot)
        if q == 1:
            send(wb.at[1 - far_q, at_x(2), y], travel[q].at[2 * TRAVEL], dev(dx=2), slot)

    def assemble(q):
        arrived(travel[q], a_slots[q])

        def put(k, block):
            cols = slice(k * blk, (k + 1) * blk)
            wz[q][z, :, cols] = (block * scr[blocks[k]]).astype(jnp.bfloat16)

        def wide(block):
            return block.astype(jnp.float32)

        along_x_, along_y_ = 0, TRAVEL
        for k, (dx, dy) in enumerate(MIRRORED):
            direct = travel[q][along_x_] if dx else wb[q, x, at_y(dy)]
            turned = travel[q][along_y_] if dy else wb[q, at_x(dx), y]
            along_x_, along_y_ = along_x_ + (dx > 0), along_y_ + (dy > 0)
            put(k, wide(direct).T + wide(turned))
        put(len(MIRRORED), wide(wb[q, x, y]).T)
        near = jnp.where(y < 2, 1.0, 0.0)
        direct = wide(wb[q, x, at_y(2)]) * near + wide(travel[q][along_x_]) * (1.0 - near)
        put(len(MIRRORED) + 1, direct.T + wide(travel[q][along_y_]))
        if q == 1:
            put(N_MAIN, wide(travel[q][2 * TRAVEL]).T + wide(wb[far_q, at_x(2), y]))

    gram[...] = jnp.zeros_like(gram)
    pairs = 2 * ri_rows * ROWS

    def contract(*units):
        units = sorted(units)
        second = [d for q, d in units if q == 1]
        main = N_MAIN * blk

        def step(i, totals):
            rows = pl.ds(pl.multiple_of(i * ROWS, ROWS), ROWS)
            b = jnp.concatenate([wz[q][at_z(d), rows, :main] for q, d in units], axis=0)
            a = mb[:, rows, :main].reshape(pairs, main)
            sums = [totals[0] + lax.dot_general(b, a, NT, preferred_element_type=jnp.float32)]
            if second:
                b = jnp.concatenate([wz1[at_z(d), rows, main:] for d in second], axis=0)
                a = mb[:, rows, main:].reshape(pairs, blk)
                sums.append(totals[1] + lax.dot_general(b, a, NT, preferred_element_type=jnp.float32))
            return sums

        heights = [ROWS * len(units)] + [ROWS * len(second)] * bool(second)
        totals = [jnp.zeros((height, pairs), jnp.float32) for height in heights]
        totals = lax.fori_loop(0, blk // ROWS, step, totals)
        places = [units, [(far_q, d) for d in second]]
        for total, where in zip(totals, places):
            i = lax.broadcasted_iota(jnp.int32, total.shape, 0) % ROWS
            j = lax.broadcasted_iota(jnp.int32, total.shape, 1) % ROWS
            total = jnp.where(i == j, total, 0.0)
            for u, (q, d) in enumerate(where):
                kept = jnp.sum(total[u * ROWS:(u + 1) * ROWS], axis=0, keepdims=True)
                row = pl.ds(4 * at_z(d) + 2 * core + q, 1)
                gram[row, :] = gram[row, :] + kept

    z_slots = [{}, {}]
    low, high = pl.ds(0, half), pl.ds(half, half)

    def z_send(q, k):
        up, down = wz[q].at[at_z(1 - k)], wz[q].at[at_z(k - 1)]
        if k < NZ // 2:
            z_slots[q][k] = send(up, up, dev(dz=1)), send(down, down, dev(dz=NZ - 1))
        else:
            slot = z_slots[q][k] = group(wz[q].at[at_z(k)])
            up, down = wz[q].at[at_z(1 - k), low], wz[q].at[at_z(k - 1), high]
            send(up, up, dev(dz=1), slot)
            send(down, down, dev(dz=NZ - 1), slot)

    def z_arrived(q, k):
        if k < NZ // 2:
            arrived(wz[q].at[at_z(-k)], z_slots[q][k][0])
            arrived(wz[q].at[at_z(k)], z_slots[q][k][1])
        else:
            arrived(wz[q].at[at_z(k)], z_slots[q][k])

    pl.semaphore_wait(barrier, len(partners))
    v_ring.start(v_ref.at[mine, v_cols])
    s_rings[0].start()
    o_ring.start(o_ref.at[mine])
    mask(1)
    for t in range(n_chunks + 3):
        if t < n_chunks:
            s_rings[t].forward()
        if t == 0:
            v_ring.forward()
            s_rings[1].start()
        if t + 2 < n_chunks:
            s_rings[t + 2].start()
        if t == 0:
            o_ring.forward()
            o_share(3)
            o_share(1)
            v_ring.finish()
            v_own.wait()
            vz_ring.start()
            o_ring.finish()
            o_share(2)
        if t == 1:
            o_join()
        if 1 <= t <= n_chunks:
            s_rings[t - 1].finish()
            left(t - 1)
            l_rings[t - 1].start()
        if t == 2:
            vz_ring.forward()
        if t == 3:
            vz_ring.finish()
            v_share()
        if 2 <= t <= n_chunks + 1:
            l_rings[t - 2].forward()
        if 3 <= t:
            l_rings[t - 3].finish()
        if t == 4:
            m_start()
        if t == CHUNKS + 2:
            v_join()
            weighted(0)
            exchange(0)
        if t == CHUNKS + 3:
            assemble(0)
            z_send(0, 1)
        if t == CHUNKS + 5:
            z_arrived(0, 1)
            z_send(0, 2)
    weighted(1)
    exchange(1)
    z_arrived(0, 2)
    z_send(0, 3)
    assemble(1)
    z_send(1, 1)
    m_join()
    contract((0, 0), (0, 7), (0, 1), (0, 6), (0, 2))
    z_arrived(0, 3)
    z_send(0, 4)
    z_arrived(1, 1)
    z_send(1, 2)
    contract((0, 5), (0, 3), (1, 0), (1, 7), (1, 1))
    flush(6)
    z_arrived(0, 4)
    z_arrived(1, 2)
    z_send(1, 3)
    contract((0, 4), (1, 6), (1, 2))
    z_arrived(1, 3)
    z_send(1, 4)
    contract((1, 5), (1, 3))
    flush(3)
    z_arrived(1, 4)
    contract((1, 4),)
    member = lax.broadcasted_iota(jnp.int32, (2 * ri_rows, pairs), 1) // ROWS
    member = member == lax.broadcasted_iota(jnp.int32, (2 * ri_rows, pairs), 0)
    part[...] = lax.dot_general(
        jnp.where(member, 1.0, 0.0), gram[...], NT, precision=lax.Precision.HIGHEST,
        preferred_element_type=jnp.float32,
    )

    own, theirs = part.at[pl.ds(0, ri_rows)], part.at[pl.ds(ri_rows, ri_rows)]
    red_x[core, x] = part[:ri_rows]
    place = red_x.at[core, x]
    slots = [send(own, place, dev(dx=d)) for d in (1, 2, 3)]
    slots += [send(theirs, place, other_core(d)) for d in range(NX)]
    for d, slot in zip((1, 2, 3), slots[:3]):
        arrived(red_x.at[core, at_x(NX - d)], slot)
    for d, slot in zip(range(NX), slots[3:]):
        arrived(red_x.at[1 - core, at_x(-d % NX)], slot)
    red_y[y] = functools.reduce(jnp.add, [red_x[i, j] for i in range(2) for j in range(NX)])
    slots = [send(red_y.at[y], red_y.at[y], dev(dy=d)) for d in (1, 2, 3)]
    for d, slot in zip((1, 2, 3), slots):
        arrived(red_y.at[at_y(NY - d)], slot)
    total = red_y[0] + red_y[1] + red_y[2] + red_y[3]
    out_ref[...] = total[:, :out_ref.shape[1]] / ao_total
    flush()


def shards(three_center, slab_tensor, occ_green, virt_green, pattern, atom_sizes):
    ri_rows, blk, ao_total = three_center.shape
    bf16, f32 = jnp.bfloat16, jnp.float32
    vmem = pl.BlockSpec(memory_space=pltpu.VMEM)
    columns = 4 * NZ
    return pl.pallas_call(
        kernel,
        out_shape=jax.ShapeDtypeStruct((ri_rows, columns), f32),
        in_specs=[pl.BlockSpec(memory_space=pl.ANY)] + [vmem] * 5,
        out_specs=vmem,
        scratch_shapes=[
            pltpu.VMEM((NX, blk, ao_total), bf16),
            pltpu.VMEM((NY, blk, ao_total), bf16),
            pltpu.VMEM((2, NY, blk, ao_total), bf16),
            pltpu.VMEM((2, NX, NY, blk, NX * blk), bf16),
            pltpu.VMEM((2, NX, NY, blk, blk), bf16),
            pltpu.VMEM((2 * TRAVEL, blk, blk), bf16),
            pltpu.VMEM((2 * TRAVEL + 1, blk, blk), bf16),
            pltpu.VMEM((NZ, blk, N_MAIN * blk), bf16),
            pltpu.VMEM((NZ, blk, N_OWNED * blk), bf16),
            pltpu.VMEM((2 * ri_rows, blk, N_OWNED * blk), bf16),
            pltpu.VMEM((NX * NY, blk, blk), f32),
            pltpu.VMEM((128, 2 * ri_rows * ROWS), f32),
            pltpu.VMEM((2 * ri_rows, 128), f32),
            pltpu.VMEM((2, NX, ri_rows, 128), f32),
            pltpu.VMEM((NY, ri_rows, 128), f32),
            pltpu.SemaphoreType.DMA((SEMS,)),
            pltpu.SemaphoreType.DMA((SEMS,)),
            pltpu.SemaphoreType.DMA((2,)),
        ],
        compiler_params=pltpu.CompilerParams(
            collective_id=0, has_side_effects=True, vmem_limit_bytes=60 * 1024 * 1024
        ),
        name="polar_slab",
    )(three_center, slab_tensor, occ_green, virt_green, pattern, atom_sizes.reshape(1, -1))


def solution(mesh):
    placed = (P("ri", "ao", None), P("ri", "ao", None), P("ao", None), P("ao", None), P(), P())
    return jax.shard_map(
        shards, mesh=mesh, in_specs=placed, out_specs=P("ri", None), check_vma=False
    )
```

time: 408 us -> 122 us (0.30)
  waiting for transfers between devices: 278 us -> 0 us
  Pallas kernels: 0 us -> 120 us
  matrix products: 56.1 us -> 0 us
  blocking collectives: 33.7 us -> 0 us
  between operations: 13.2 us -> 0.01 us
  local copies, waits for them, and re-layouts: 12.4 us -> 1.3 us
  other arithmetic: 10.2 us -> 0 us
    all_gather x3 -> x0, waiting for transfers between devices: 278 us -> none  [the longest x1 119 us: shards(): shard_piece = lax.all_gather(slab_masked, 'ao', axis=1, tiled=True)]
    pallas_call x0 -> x1, Pallas kernels: none -> 120 us  [shards(): pl.pallas_call(kernel, out_shape=jax.ShapeDtypeStruct((ri_rows, columns),...]
    dot_general x3 -> x0, matrix products: 56.1 us -> none  [the longest x1 41.2 us: shards(): lax.dot_general(flattened, shard_piece.reshape(piece_rows, own_rows * ao_...]
    psum x1 -> x0, blocking collectives: 33.7 us -> none  [shards(): return lax.psum(columns_part, 'ao') / ao_total]
    mul x2 -> x0, other arithmetic: 8.62 us -> none  [the longest x1 7.44 us: shards(): masked = three_center * screen[None]]
    convert_element_type x2 -> x0, local copies, waits for them, and re-layouts: 7.95 us -> none  [the longest x1 7.87 us: expand_pattern(): grown.reshape(row_atoms * ATOM_BS, col_atoms * ATOM_BS).astype(jnp.float32)]
    broadcast_in_dim x1 -> x0, local copies, waits for them, and re-layouts: 4.33 us -> none  [expand_pattern(): jnp.broadcast_to(pattern_rows[:, None, :, None], (row_atoms, ATOM_BS, col...]
  transfers between devices with their start and end apart: 3 -> 0, of which waited for: 3 -> 0; matrix products, arithmetic and copies ran while one was open for 4% -> 0% of each run, Pallas kernels for 0% -> 0%
where the time goes in v2:
time: 122 us
  Pallas kernels  120 us (98%)
  local copies, waits for them, and re-layouts  1.3 us (1%)
    pallas_call x1, Pallas kernels, shards(): pl.pallas_call(kernel, out_shape=jax.ShapeDtypeStruct((ri_rows, columns),...  120 us

profile of v2, /device:TPU:1, one launch (start us, length us, event | category | flops | bytes accessed | tf_op | source)
XLA Modules:
  0.0 121.6 jit_solution(15463039663094345969)
XLA Ops:
  0.0 120.3 %polar_slab.1 = f32[16,32]{1,0:T(8,128)} custom-call(bf16[16,128,2048]{2,1,0:T(8,128)(2,1)} %m_ref.1, bf16[2,128,2048]{2,1,0:T(8,128)(2,1)} %s_ref.1, bf16[128,2048]{1,0:T(8,128)(2,1)} %o_ref.1, bf16[128,2048]{1,0:T(8,128)(2,1)} %v_ref.1, s32[128,128]{1,0:T(8,128)} %pat_ref.1, s32[1,128]{1,0:T(1,128)} %bitcast.1), custom_call_target="tpu_custom_call" | custom-call | tf_op jit(solution)/shard_map/polar_slab/pallas_call | solution.py:420
  120.3 1.3 %copy.8 = f32[16,32]{1,0:T(8,128)} copy(f32[16,32]{1,0:T(8,128)} %polar_slab.1) | data formatting | bytes 4096

commit v3 on v2

--- a/solution.py
+++ b/solution.py
@@ -12,10 +12,10 @@
 NX, NY, NZ = 4, 4, 8
 ROWS = 16
 CHUNKS = 4
-SEMS = 96
+ARRIVALS, BOXES = 87, 14
 V_PARTS = 4
 
-MIRRORED = ((1, 0), (3, 3), (1, 3), (3, 2), (0, 1), (2, 1))
+MIRRORED = ((1, 0), (1, 1), (1, 3), (1, 2), (0, 1), (2, 1))
 N_MAIN = len(MIRRORED) + 2
 N_OWNED = N_MAIN + 1
 TRAVEL = 6
@@ -52,34 +52,34 @@
     half = blk // 2
     mine = pl.ds(pl.multiple_of(core * half, half), half)
 
-    sent = []
-
-    def remote(src, dst, device, slot):
+    landed, boxes, emptied = [0], [], [0]
+
+    def remote(src, dst, device, slot, box):
         return pltpu.make_async_remote_copy(
-            src_ref=src, dst_ref=dst, send_sem=ssem.at[slot], recv_sem=rsem.at[slot],
+            src_ref=src, dst_ref=dst, send_sem=ssem.at[box], recv_sem=rsem.at[slot],
             device_id=device, device_id_type=MESH,
         )
 
-    def group(whole):
-        sent.append(remote(whole, whole, sibling, len(sent)))
-        return len(sent) - 1
-
-    def send(src, dst, device, slot=None):
-        if slot is None:
-            slot = len(sent)
-            sent.append(remote(src, dst, device, slot))
-        remote(src, dst, device, slot).start()
+    def outbox(whole):
+        boxes.append(whole)
+        return len(boxes) - 1
+
+    def take():
+        landed[0] += 1
+        return landed[0] - 1
+
+    def send(src, dst, device, box, slot=None):
+        slot = take() if slot is None else slot
+        remote(src, dst, device, slot, box).start()
         return slot
 
-    flushed = [0]
-
-    def flush(keep=0):
-        for copy in sent[flushed[0]:len(sent) - keep]:
-            copy.wait_send()
-        flushed[0] = len(sent) - keep
+    def flush(last=None):
+        for box in range(emptied[0], len(boxes) if last is None else last + 1):
+            remote(boxes[box], boxes[box], sibling, 0, box).wait_send()
+            emptied[0] = box + 1
 
     def arrived(ref, slot):
-        remote(ref, ref, sibling, slot).wait_recv()
+        remote(ref, ref, sibling, slot, 0).wait_recv()
 
     barrier = pltpu.get_barrier_semaphore()
     partners = [dev(dx=1), dev(dx=2), dev(dx=3), dev(dy=1), dev(dy=2), dev(dy=3), sibling]
@@ -89,8 +89,8 @@
         pl.semaphore_signal(barrier, inc=1, device_id=partner, device_id_type=MESH)
 
     class Ring:
-        def __init__(self, view, at, device, rows, start=0):
-            self.view, self.at, self.device = view, at, device
+        def __init__(self, view, at, device, box, rows, start=0):
+            self.view, self.at, self.device, self.box = view, at, device, box
             self.low = pl.ds(start, rows // 2)
             self.high = pl.ds(start + rows // 2, rows // 2)
             self.all = pl.ds(start, rows)
@@ -98,17 +98,16 @@
         def start(self, src=None):
             block = self.view(self.at(0), self.all)
             src = block if src is None else src
-            self.a = send(src, block, self.device(1))
-            self.b = send(src, block, self.device(3))
+            self.a = send(src, block, self.device(1), self.box)
+            self.b = send(src, block, self.device(3), self.box)
 
         def forward(self):
             arrived(self.view(self.at(3), self.all), self.a)
             piece = self.view(self.at(3), self.low)
-            self.c = group(self.view(self.at(2), self.all))
-            send(piece, piece, self.device(1), self.c)
+            self.c = send(piece, piece, self.device(1), self.box)
             arrived(self.view(self.at(1), self.all), self.b)
             piece = self.view(self.at(1), self.high)
-            send(piece, piece, self.device(3), self.c)
+            send(piece, piece, self.device(3), self.box, self.c)
 
         def finish(self):
             arrived(self.view(self.at(2), self.all), self.c)
@@ -130,18 +129,26 @@
     c_rows = blk // CHUNKS
     n_chunks = 2 * CHUNKS
 
-    o_ring = Ring(lambda i, r: oh.at[i, r], at_x, along_x, half, base)
-    v_ring = Ring(lambda i, r: vn.at[i, r, v_cols], at_y, along_y, half, base)
+    quarter = half // 2
+    o_box = outbox(oh.at[pl.ds(0, 3)])
+    o_rings = [
+        Ring(lambda i, r: oh.at[i, r], at_x, along_x, o_box, quarter, base + part_ * quarter) for part_ in range(2)
+    ]
+    v_ring = Ring(
+        lambda i, r: vn.at[i, r, v_cols], at_y, along_y, outbox(vn.at[pl.ds(0, 3), mine, v_cols]), half, base
+    )
     vz_ring = Ring(
         lambda i, r: vn.at[:, r, v_part(i)], lambda d: (z + d) % V_PARTS,
-        lambda d: dev(dz=1 if d == 1 else NZ - 1), half, base,
+        lambda d: dev(dz=1 if d == 1 else NZ - 1), outbox(vn.at[:, mine, pl.ds(0, 3 * v_width)]), half, base,
     )
+    v_box = outbox(vn.at[:, mine])
+    s_box, l_box = outbox(sg.at[:, pl.ds(0, 3)]), outbox(lb.at[:, pl.ds(0, 3)])
     s_rings, l_rings = [], []
     for t in range(n_chunks):
         q, start = t // CHUNKS, t % CHUNKS * c_rows
-        s_rings.append(Ring(lambda i, r, q=q: sg.at[q, i, r], at_y, along_y, c_rows, start))
+        s_rings.append(Ring(lambda i, r, q=q: sg.at[q, i, r], at_y, along_y, s_box, c_rows, start))
         l_rings.append(
-            Ring(lambda i, r, q=q, start=start: lb.at[q, i, r, pl.ds(start, c_rows)], at_x, along_x, NY)
+            Ring(lambda i, r, q=q, start=start: lb.at[q, i, r, pl.ds(start, c_rows)], at_x, along_x, l_box, NY)
         )
 
     atoms = pat_ref.shape[0]
@@ -170,17 +177,19 @@
 
     o_slots, v_slots, m_slots = [], [], []
 
-    def o_share(d):
-        piece = oh.at[at_x(d), mine]
-        o_slots.append(send(piece, piece, sibling))
+    def o_share(part_, d):
+        piece = oh.at[at_x(d), pl.ds(base + part_ * quarter, quarter)]
+        o_slots.append((part_, d, send(piece, piece, sibling, o_box)))
 
     def o_join():
-        for d, slot in zip((3, 1, 2), o_slots):
-            arrived(oh.at[at_x(d), other], slot)
+        start = (1 - core) * half
+        for part_, d, slot in o_slots:
+            rows = pl.ds(pl.multiple_of(start + part_ * quarter, quarter), quarter)
+            arrived(oh.at[at_x(d), rows], slot)
 
     def v_share():
         piece = vn.at[:, mine]
-        v_slots.append(send(piece, piece, sibling))
+        v_slots.append(send(piece, piece, sibling, v_box))
 
     def v_join():
         arrived(vn.at[:, other], v_slots[-1])
@@ -192,12 +201,13 @@
     m_own, m_other = mb.at[pl.ds(0, ri_rows)], mb.at[pl.ds(ri_rows, ri_rows)]
 
     def m_start():
-        m_slots.append(group(m_other))
+        m_slots.append(take())
+        box = outbox(m_other)
         for k, b in enumerate(blocks):
             src = m_ref.at[:, :, pl.ds(pl.multiple_of(b * blk, blk), blk)]
             cols = pl.ds(k * blk, blk)
             pltpu.make_async_copy(src, mb.at[pl.ds(0, ri_rows), :, cols], lsem.at[0]).start()
-            send(src, mb.at[pl.ds(ri_rows, ri_rows), :, cols], sibling, m_slots[0])
+            send(src, mb.at[pl.ds(ri_rows, ri_rows), :, cols], sibling, box, m_slots[0])
 
     def m_join():
         pltpu.make_async_copy(m_own, m_own, lsem.at[0]).wait()
@@ -225,19 +235,20 @@
     wz = (wz0, wz1)
 
     def exchange(q):
-        slot = a_slots[q] = group(travel[q])
+        slot, box = take(), outbox(travel[q])
+        a_slots[q] = slot
         along_x_, along_y_ = 0, TRAVEL
         for dx, dy in MIRRORED:
             if dx:
-                send(wb.at[q, at_x(NX - dx), at_y(dy)], travel[q].at[along_x_], dev(dx=NX - dx), slot)
+                send(wb.at[q, at_x(NX - dx), at_y(dy)], travel[q].at[along_x_], dev(dx=NX - dx), box, slot)
                 along_x_ += 1
             if dy:
-                send(wb.at[q, at_x(dx), at_y(NY - dy)], travel[q].at[along_y_], dev(dy=NY - dy), slot)
+                send(wb.at[q, at_x(dx), at_y(NY - dy)], travel[q].at[along_y_], dev(dy=NY - dy), box, slot)
                 along_y_ += 1
-        send(wb.at[q, at_x(2), at_y(2)], travel[q].at[along_x_], dev(dx=2), slot)
-        send(wb.at[q, at_x(2 - 2 * (y // 2)), at_y(2)], travel[q].at[along_y_], dev(dy=2), slot)
+        send(wb.at[q, at_x(2), at_y(2)], travel[q].at[along_x_], dev(dx=2), box, slot)
+        send(wb.at[q, at_x(2 - 2 * (y // 2)), at_y(2)], travel[q].at[along_y_], dev(dy=2), box, slot)
         if q == 1:
-            send(wb.at[1 - far_q, at_x(2), y], travel[q].at[2 * TRAVEL], dev(dx=2), slot)
+            send(wb.at[1 - far_q, at_x(2), y], travel[q].at[2 * TRAVEL], dev(dx=2), box, slot)
 
     def assemble(q):
         arrived(travel[q], a_slots[q])
@@ -283,7 +294,7 @@
 
         heights = [ROWS * len(units)] + [ROWS * len(second)] * bool(second)
         totals = [jnp.zeros((height, pairs), jnp.float32) for height in heights]
-        totals = lax.fori_loop(0, blk // ROWS, step, totals)
+        totals = lax.fori_loop(0, blk // ROWS, step, totals, unroll=True)
         places = [units, [(far_q, d) for d in second]]
         for total, where in zip(totals, places):
             i = lax.broadcasted_iota(jnp.int32, total.shape, 0) % ROWS
@@ -294,61 +305,74 @@
                 row = pl.ds(4 * at_z(d) + 2 * core + q, 1)
                 gram[row, :] = gram[row, :] + kept
 
-    z_slots = [{}, {}]
+    z_slots, z_boxes = [{}, {}], [None, None]
     low, high = pl.ds(0, half), pl.ds(half, half)
 
-    def z_send(q, k):
-        up, down = wz[q].at[at_z(1 - k)], wz[q].at[at_z(k - 1)]
-        if k < NZ // 2:
-            z_slots[q][k] = send(up, up, dev(dz=1)), send(down, down, dev(dz=NZ - 1))
-        else:
-            slot = z_slots[q][k] = group(wz[q].at[at_z(k)])
-            up, down = wz[q].at[at_z(1 - k), low], wz[q].at[at_z(k - 1), high]
-            send(up, up, dev(dz=1), slot)
-            send(down, down, dev(dz=NZ - 1), slot)
-
-    def z_arrived(q, k):
-        if k < NZ // 2:
-            arrived(wz[q].at[at_z(-k)], z_slots[q][k][0])
-            arrived(wz[q].at[at_z(k)], z_slots[q][k][1])
-        else:
-            arrived(wz[q].at[at_z(k)], z_slots[q][k])
+    halves = (low, high)
+
+    def z_send(q, k, h):
+        if (k, h) == (1, 0):
+            z_boxes[q] = outbox(wz[q].at[pl.ds(0, NZ - 1)])
+        box, last = z_boxes[q], k == NZ // 2
+        slot = z_slots[q][k, h] = z_slots[q][k, 0] if last and h else take()
+        up, down = wz[q].at[at_z(1 - k), halves[h]], wz[q].at[at_z(k - 1), halves[h]]
+        if not last or h == 0:
+            send(up, up, dev(dz=1), box, slot)
+        if not last or h == 1:
+            send(down, down, dev(dz=NZ - 1), box, slot)
+
+    def z_arrived(q, k, h=0):
+        arrived(wz[q].at[at_z(k)], z_slots[q][k, h])
+
+    def z_step(q, k, h):
+        z_arrived(q, k, h)
+        z_send(q, k + 1, h)
 
     pl.semaphore_wait(barrier, len(partners))
     v_ring.start(v_ref.at[mine, v_cols])
     s_rings[0].start()
-    o_ring.start(o_ref.at[mine])
+    for part_ in range(2):
+        rows = pl.ds(pl.multiple_of(base + part_ * quarter, quarter), quarter)
+        o_rings[part_].start(o_ref.at[rows])
+    s_rings[1].start()
     mask(1)
+    o_rings[0].forward()
     for t in range(n_chunks + 3):
         if t < n_chunks:
             s_rings[t].forward()
         if t == 0:
             v_ring.forward()
-            s_rings[1].start()
         if t + 2 < n_chunks:
             s_rings[t + 2].start()
         if t == 0:
-            o_ring.forward()
-            o_share(3)
-            o_share(1)
-            v_ring.finish()
-            v_own.wait()
-            vz_ring.start()
-            o_ring.finish()
-            o_share(2)
+            o_share(0, 3)
+            o_share(0, 1)
+            o_rings[1].forward()
+            o_share(1, 3)
+            o_share(1, 1)
+            o_rings[0].finish()
+            o_share(0, 2)
+            o_rings[1].finish()
+            o_share(1, 2)
         if t == 1:
             o_join()
         if 1 <= t <= n_chunks:
             s_rings[t - 1].finish()
             left(t - 1)
             l_rings[t - 1].start()
-        if t == 2:
+        if t == 1:
+            v_ring.finish()
+            v_own.wait()
+            vz_ring.start()
+        if t == 3:
             vz_ring.forward()
-        if t == 3:
+        if t == 4:
             vz_ring.finish()
             v_share()
         if 2 <= t <= n_chunks + 1:
             l_rings[t - 2].forward()
+        if t == CHUNKS + 6:
+            z_step(0, 2, 0)
         if 3 <= t:
             l_rings[t - 3].finish()
         if t == 4:
@@ -359,32 +383,34 @@
             exchange(0)
         if t == CHUNKS + 3:
             assemble(0)
-            z_send(0, 1)
+            z_send(0, 1, 0)
+            z_send(0, 1, 1)
+        if t == CHUNKS + 4:
+            z_step(0, 1, 0)
         if t == CHUNKS + 5:
-            z_arrived(0, 1)
-            z_send(0, 2)
+            z_step(0, 1, 1)
     weighted(1)
     exchange(1)
-    z_arrived(0, 2)
-    z_send(0, 3)
+    z_step(0, 2, 1)
     assemble(1)
-    z_send(1, 1)
+    z_send(1, 1, 0)
+    z_send(1, 1, 1)
     m_join()
     contract((0, 0), (0, 7), (0, 1), (0, 6), (0, 2))
-    z_arrived(0, 3)
-    z_send(0, 4)
-    z_arrived(1, 1)
-    z_send(1, 2)
+    z_step(0, 3, 0)
+    z_step(0, 3, 1)
+    z_step(1, 1, 0)
+    z_step(1, 1, 1)
     contract((0, 5), (0, 3), (1, 0), (1, 7), (1, 1))
-    flush(6)
+    flush(z_boxes[0] - 1)
+    z_step(1, 2, 0)
     z_arrived(0, 4)
-    z_arrived(1, 2)
-    z_send(1, 3)
+    z_step(1, 2, 1)
     contract((0, 4), (1, 6), (1, 2))
-    z_arrived(1, 3)
-    z_send(1, 4)
+    z_step(1, 3, 0)
+    z_step(1, 3, 1)
     contract((1, 5), (1, 3))
-    flush(3)
+    flush(z_boxes[0])
     z_arrived(1, 4)
     contract((1, 4),)
     member = lax.broadcasted_iota(jnp.int32, (2 * ri_rows, pairs), 1) // ROWS
@@ -397,19 +423,23 @@
     own, theirs = part.at[pl.ds(0, ri_rows)], part.at[pl.ds(ri_rows, ri_rows)]
     red_x[core, x] = part[:ri_rows]
     place = red_x.at[core, x]
-    slots = [send(own, place, dev(dx=d)) for d in (1, 2, 3)]
-    slots += [send(theirs, place, other_core(d)) for d in range(NX)]
-    for d, slot in zip((1, 2, 3), slots[:3]):
-        arrived(red_x.at[core, at_x(NX - d)], slot)
-    for d, slot in zip(range(NX), slots[3:]):
-        arrived(red_x.at[1 - core, at_x(-d % NX)], slot)
+    near, far = take(), take()
+    near_box, far_box = outbox(red_x.at[0, pl.ds(0, 3)]), outbox(red_x.at[0])
+    for d in (1, 2, 3):
+        send(own, place, dev(dx=d), near_box, near)
+    for d in range(NX):
+        send(theirs, place, other_core(d), far_box, far)
+    arrived(red_x.at[core, pl.ds(0, 3)], near)
+    arrived(red_x.at[1 - core], far)
     red_y[y] = functools.reduce(jnp.add, [red_x[i, j] for i in range(2) for j in range(NX)])
-    slots = [send(red_y.at[y], red_y.at[y], dev(dy=d)) for d in (1, 2, 3)]
-    for d, slot in zip((1, 2, 3), slots):
-        arrived(red_y.at[at_y(NY - d)], slot)
+    slot, box = take(), outbox(red_y.at[pl.ds(0, 3)])
+    for d in (1, 2, 3):
+        send(red_y.at[y], red_y.at[y], dev(dy=d), box, slot)
+    arrived(red_y.at[pl.ds(0, 3)], slot)
     total = red_y[0] + red_y[1] + red_y[2] + red_y[3]
     out_ref[...] = total[:, :out_ref.shape[1]] / ao_total
     flush()
+    assert (landed[0], len(boxes)) == (ARRIVALS, BOXES), (landed, len(boxes))
 
 
 def shards(three_center, slab_tensor, occ_green, virt_green, pattern, atom_sizes):
@@ -438,8 +468,8 @@
             pltpu.VMEM((2 * ri_rows, 128), f32),
             pltpu.VMEM((2, NX, ri_rows, 128), f32),
             pltpu.VMEM((NY, ri_rows, 128), f32),
-            pltpu.SemaphoreType.DMA((SEMS,)),
-            pltpu.SemaphoreType.DMA((SEMS,)),
+            pltpu.SemaphoreType.DMA((BOXES,)),
+            pltpu.SemaphoreType.DMA((ARRIVALS,)),
             pltpu.SemaphoreType.DMA((2,)),
         ],
         compiler_params=pltpu.CompilerParams(

time: 122 us -> 115 us (0.943)
  Pallas kernels: 120 us -> 114 us
    pallas_call x1, Pallas kernels: 120 us -> 114 us  [shards(): pl.pallas_call(kernel, out_shape=jax.ShapeDtypeStruct((ri_rows, columns),...]
where the time goes in v3:
time: 115 us
  Pallas kernels  114 us (99%)
  local copies, waits for them, and re-layouts  1.3 us (1%)
    pallas_call x1, Pallas kernels, shards(): pl.pallas_call(kernel, out_shape=jax.ShapeDtypeStruct((ri_rows, columns),...  114 us

profile of v3, /device:TPU:1, one launch (start us, length us, event | category | flops | bytes accessed | tf_op | source)
XLA Modules:
  0.0 114.9 jit_solution(12743349999430085814)
XLA Ops:
  0.0 113.6 %polar_slab.1 = f32[16,32]{1,0:T(8,128)} custom-call(bf16[16,128,2048]{2,1,0:T(8,128)(2,1)} %m_ref.1, bf16[2,128,2048]{2,1,0:T(8,128)(2,1)} %s_ref.1, bf16[128,2048]{1,0:T(8,128)(2,1)} %o_ref.1, bf16[128,2048]{1,0:T(8,128)(2,1)} %v_ref.1, s32[128,128]{1,0:T(8,128)} %pat_ref.1, s32[1,128]{1,0:T(1,128)} %bitcast.1), custom_call_target="tpu_custom_call" | custom-call | tf_op jit(solution)/shard_map/polar_slab/pallas_call | solution.py:450
  113.6 1.3 %copy.8 = f32[16,32]{1,0:T(8,128)} copy(f32[16,32]{1,0:T(8,128)} %polar_slab.1) | data formatting | bytes 4096

commit v4 on v3

--- a/solution.py
+++ b/solution.py
@@ -392,12 +392,12 @@
     weighted(1)
     exchange(1)
     z_step(0, 2, 1)
+    z_step(0, 3, 0)
     assemble(1)
     z_send(1, 1, 0)
     z_send(1, 1, 1)
     m_join()
     contract((0, 0), (0, 7), (0, 1), (0, 6), (0, 2))
-    z_step(0, 3, 0)
     z_step(0, 3, 1)
     z_step(1, 1, 0)
     z_step(1, 1, 1)

time: 115 us -> 114 us (level)
  no operation moved by 1% of the time
where the time goes in v4:
time: 114 us
  Pallas kernels  113 us (99%)
  local copies, waits for them, and re-layouts  1.3 us (1%)
    pallas_call x1, Pallas kernels, shards(): pl.pallas_call(kernel, out_shape=jax.ShapeDtypeStruct((ri_rows, columns),...  113 us

profile of v4, /device:TPU:1, one launch (start us, length us, event | category | flops | bytes accessed | tf_op | source)
XLA Modules:
  0.0 113.8 jit_solution(6710328879852953842)
XLA Ops:
  0.0 112.5 %polar_slab.1 = f32[16,32]{1,0:T(8,128)} custom-call(bf16[16,128,2048]{2,1,0:T(8,128)(2,1)} %m_ref.1, bf16[2,128,2048]{2,1,0:T(8,128)(2,1)} %s_ref.1, bf16[128,2048]{1,0:T(8,128)(2,1)} %o_ref.1, bf16[128,2048]{1,0:T(8,128)(2,1)} %v_ref.1, s32[128,128]{1,0:T(8,128)} %pat_ref.1, s32[1,128]{1,0:T(1,128)} %bitcast.1), custom_call_target="tpu_custom_call" | custom-call | tf_op jit(solution)/shard_map/polar_slab/pallas_call | solution.py:450
  112.5 1.3 %copy.8 = f32[16,32]{1,0:T(8,128)} copy(f32[16,32]{1,0:T(8,128)} %polar_slab.1) | data formatting | bytes 4096
